TPU v7x, 512 devices: a whole 4x8x8 slice. The times are simulated.
512 devices in a mesh: dp: 32 (over x, y), seq: 16 (over z, core).
Axes of the slice: x: 4, y: 8, z: 8, core: 2. Of those that a mesh axis runs over, the one named last changes fastest.
Arguments:
- volume: bfloat16 [32, 3072, 1024], P('dp', 'seq')
- cotangent: bfloat16 [32, 3072, 1024], P('dp', 'seq'), may hold values from -6 to 6
- weights: bfloat16 [1024, 3, 1024], P('dp')
- pairs: int32 [32, 16, 24, 4], P('dp', 'seq'), may hold values from 0 to 23, as said below
- valid: int32 [32, 16, 24, 4], P('dp', 'seq'), may hold values from 0 to 1, as said below
Outputs:
- attended: bfloat16 [32, 3072, 1024], P('dp', 'seq')
- weight_grad: float32 [1024, 3, 1024], P('dp', None, 'seq')
Inputs may be any that keep to these rules, and one draw needn't show every extreme that they name: `pairs`: slot 0 of query block b holds b; the key blocks of one query block's slots are distinct. `valid`: slot 0 is always 1.
All inputs are finite; a program needn't handle non-finite values.
Results may differ from a plain program's by a relative error of at most 0.03.
Values may be sent and summed in bfloat16 or wider, within the bound.
No kernel may reach another device: no remote copies, remote signals or barrier semaphores. Data moves between devices by JAX's collectives and lax.ppermute only.
A program may use at most 64 MiB of HBM per device.

v0:
```python
import math
import jax
import jax.numpy as jnp
from jax import lax
from jax.sharding import PartitionSpec as P

HD = 64


def head_pass(queries, keys_all, values_all, upstream, pair_list, pair_live):
    block_count, slot_count = pair_list.shape
    all_rows, head_size = queries.shape
    block_rows = all_rows // block_count
    per_step = math.gcd(block_count, max(1, 512 // block_rows))
    steps_n = block_count // per_step
    scaling = head_size ** (-0.5)
    key_blocks = keys_all.reshape(block_count, block_rows, head_size)
    value_blocks = values_all.reshape(block_count, block_rows, head_size)
    block_index = jnp.arange(block_count, dtype=jnp.int32)

    def step(totals, sliced):
        key_total, value_total = totals
        query_rows, grad_rows, slot_blocks, slot_live = sliced
        key_rows = key_blocks[slot_blocks].reshape(per_step, slot_count * block_rows, head_size)
        value_rows = value_blocks[slot_blocks].reshape(per_step, slot_count * block_rows, head_size)
        live_cols = jnp.repeat(slot_live > 0, block_rows, axis=1)[:, None, :]
        scores = (
            jnp.einsum("nqd,nkd->nqk", query_rows, key_rows, preferred_element_type=jnp.float32)
            * scaling
        )
        row_max = jnp.max(jnp.where(live_cols, scores, -1e30), axis=-1, keepdims=True)
        exponent = jnp.where(live_cols, jnp.exp(scores - row_max), 0.0)
        prob_full = exponent / jnp.sum(exponent, axis=-1, keepdims=True)
        rounded = prob_full.astype(jnp.bfloat16)
        result = jnp.einsum(
            "nqk,nkd->nqd", rounded, value_rows, preferred_element_type=jnp.float32
        ).astype(jnp.bfloat16)
        value_grad = jnp.einsum(
            "nqk,nqd->nkd", rounded, grad_rows, preferred_element_type=jnp.float32
        )
        prob_grad = jnp.einsum(
            "nqd,nkd->nqk", grad_rows, value_rows, preferred_element_type=jnp.float32
        )
        row_dot = jnp.sum(
            grad_rows.astype(jnp.float32) * result.astype(jnp.float32), axis=-1, keepdims=True
        )
        score_grad = (prob_full * (prob_grad - row_dot) * scaling).astype(jnp.bfloat16)
        query_grad = jnp.einsum(
            "nqk,nkd->nqd", score_grad, key_rows, preferred_element_type=jnp.float32
        ).astype(jnp.bfloat16)
        key_grad = jnp.einsum(
            "nqk,nqd->nkd", score_grad, query_rows, preferred_element_type=jnp.float32
        )
        one_hot = (
            (slot_blocks.reshape(-1)[:, None] == block_index[None, :])
            & (slot_live.reshape(-1)[:, None] > 0)
        ).astype(jnp.float32)
        key_total = key_total + jnp.einsum(
            "jb,jrd->brd",
            one_hot,
            key_grad.reshape(per_step * slot_count, block_rows, head_size),
            precision=lax.Precision.HIGHEST,
        )
        value_total = value_total + jnp.einsum(
            "jb,jrd->brd",
            one_hot,
            value_grad.reshape(per_step * slot_count, block_rows, head_size),
            precision=lax.Precision.HIGHEST,
        )
        return ((key_total, value_total), (result, query_grad))

    empty_acc = jnp.zeros((block_count, block_rows, head_size), jnp.float32)
    sliced_all = (
        queries.reshape(steps_n, per_step, block_rows, head_size),
        upstream.reshape(steps_n, per_step, block_rows, head_size),
        pair_list.reshape(steps_n, per_step, slot_count),
        pair_live.reshape(steps_n, per_step, slot_count),
    )
    (key_total, value_total), (results, query_grads) = lax.scan(
        step, (empty_acc, empty_acc), sliced_all
    )
    return (
        results.reshape(all_rows, head_size),
        query_grads.reshape(all_rows, head_size),
        key_total.astype(jnp.bfloat16).reshape(all_rows, head_size),
        value_total.astype(jnp.bfloat16).reshape(all_rows, head_size),
    )


def local(volume, cotangent, weights, pairs, valid):
    seq_devices = lax.axis_size("seq")
    local_volume = volume[0]
    local_grad = cotangent[0]
    tok_count = local_volume.shape[0]
    width_all = local_grad.shape[1]
    local_cols = width_all // seq_devices
    all_rows = tok_count * seq_devices
    projected = jnp.einsum(
        "td,djc->tjc",
        local_volume,
        lax.all_gather(weights, "dp", axis=0, tiled=True),
        preferred_element_type=jnp.float32,
    )
    projected = projected.astype(jnp.bfloat16)
    head_inputs, head_grad = (
        lax.all_to_all(projected, "seq", split_axis=2, concat_axis=0, tiled=True),
        lax.all_to_all(
            local_grad.reshape(tok_count, 1, width_all),
            "seq",
            split_axis=2,
            concat_axis=0,
            tiled=True,
        ),
    )
    head_grad = head_grad.reshape(all_rows, local_cols)
    upper = HD
    result, query_grad, key_grad, value_grad = head_pass(
        head_inputs[:, 0, 0:upper],
        head_inputs[:, 1, 0:upper],
        head_inputs[:, 2, 0:upper],
        head_grad,
        pairs[0, 0],
        valid[0, 0],
    )
    grad_flat = jnp.stack([query_grad, key_grad, value_grad], axis=1).reshape(
        all_rows, 3 * local_cols
    )
    attended = lax.all_to_all(result, "seq", split_axis=0, concat_axis=1, tiled=True)
    local_sum = lax.dot_general(
        lax.all_gather(local_volume, "seq", axis=0, tiled=True),
        grad_flat,
        (((0,), (0,)), ((), ())),
        preferred_element_type=jnp.float32,
    )
    weight_part = (
        lax.psum_scatter(local_sum.astype(jnp.bfloat16), "dp", scatter_dimension=0, tiled=True)
        .astype(jnp.float32)
        .reshape(-1, 3, local_cols)
    )
    return (attended[None], weight_part)


def solution(mesh):
    return jax.shard_map(
        local,
        mesh=mesh,
        in_specs=(
            P("dp", "seq", None),
            P("dp", "seq", None),
            P("dp", None, None),
            P("dp", "seq", None, None),
            P("dp", "seq", None, None),
        ),
        out_specs=(P("dp", "seq", None), P("dp", None, "seq")),
        check_vma=False,
    )
```

profile of v0, /device:TPU:16, one launch (start us, length us, event | category | flops | bytes accessed | tf_op | source)
XLA Modules:
  0.0 509.1 jit_solution(6228003603930186872)
XLA Ops:
  8.7 2.4 copy.66
  11.6 4.1 reduce
  17.1 10.4 %all-to-all-start.1 = ((bf16[16,2,6144]{2,1,0:T(2,128)(2,1)}), bf16[16,2,6144]{2,1,0:T(2,128)(2,1)S(1)}, u32[]{:S(2)}, u32[]{:S(2)}) async-start(bf16[16,2,6144]{2,1,0:T(2,128)(2,1)} %reshape.121), calls=%async_computation.1 | async-start | bytes 786432 | tf_op jit(solution)/shard_map/all_to_all | solution.py:107
  27.5 81.9 %all-gather.4.cloned.1.call-done = bf16[1024,3,1024]{2,0,1:T(8,128)(2,1)} async-done(((bf16[32,3,1024]{2,0,1:T(8,128)(2,1)}), bf16[1024,3,1024]{2,0,1:T(8,128)(2,1)}) %all-gather.4.cloned.1.call-update) | async-done | bytes 6291472 | tf_op jit(solution)/shard_map/all_gather | solution.py:101
  109.4 4.2 convolution_convert_fusion.2
  113.6 2.6 copy.63
  116.2 7.6 %all-to-all-start = ((bf16[192,3,1024]{0,1,2:T(4,128)(2,1)}), bf16[192,3,1024]{0,1,2:T(4,128)(2,1)S(1)}, u32[]{:S(2)}, u32[]{:S(2)}) async-start(bf16[192,3,1024]{0,1,2:T(4,128)(2,1)} %copy.63), calls=%async_computation | async-start | bytes 4194304 | tf_op jit(solution)/shard_map/all_to_all | solution.py:106
  125.4 2.0 reshape.122
  130.4 57.3 %all-to-all-done = bf16[192,3,1024]{0,1,2:T(4,128)(2,1)S(1)} async-done(((bf16[192,3,1024]{0,1,2:T(4,128)(2,1)}), bf16[192,3,1024]{0,1,2:T(4,128)(2,1)S(1)}, u32[]{:S(2)}, u32[]{:S(2)}) %all-to-all-start) | async-done | bytes 1179680 | tf_op jit(solution)/shard_map/all_to_all | solution.py:106
  194.0 83.2 %while.17 = (s32[]{:T(128)}, f32[24,128,64]{1,0,2:T(8,128)S(1)}, f32[24,128,64]{1,0,2:T(8,128)}, bf16[6,4,128,64]{2,1,0,3:T(4,128)(2,1)}, bf16[6,4,128,64]{2,1,0...) while((s32[]{:T(128)}, f32[24,128,64]{1,0,2:T(8,128)S(1)}, ...), condition=%wide.region_4.5_spmd.clone, body=%wide.region_0.4_spmd.clone.sunk | while | flops 280955456 | bytes 27224828 | solution.py:79
  194.7 1.8 gather_fusion.1
  198.9 1.8 gather_fusion
  208.7 1.8 gather_fusion.1
  212.8 1.8 gather_fusion
  222.5 1.8 gather_fusion.1
  226.7 1.8 gather_fusion
  236.4 1.8 gather_fusion.1
  240.5 1.8 gather_fusion
  250.2 1.8 gather_fusion.1
  254.4 1.8 gather_fusion
  268.2 1.8 gather_fusion
  279.0 4.2 fusion.34
  284.8 23.0 %all_to_all.49 = bf16[16,192,64]{1,2,0:T(8,128)(2,1)S(1)} all-to-all(bf16[16,192,64]{1,2,0:T(8,128)(2,1)S(1)} %copy.75), channel_id=1, replica_groups=mesh['dp'=32,'seq'=16] {'seq'}, dimensions={0} | all-to-all | bytes 786432 | tf_op jit(solution)/shard_map/all_to_all | solution.py:128
  308.7 191.4 %reduce-scatter.4.cloned.1.call-done = bf16[32,192]{1,0:T(8,128)(2,1)} async-done(((bf16[1024,192]{1,0:T(8,128)(2,1)}), bf16[32,192]{1,0:T(8,128)(2,1)}) %reduce-scatter.4.cloned.1.call-update) | async-done | bytes 12304
  (255 shorter events, 81.9 us)
Async XLA Ops:
  8.0 101.4 %all-gather.4.cloned.1.call-start = ((), (), s32[]{:S(2)}) async-start(), calls=%async_computation.4 | async-start | bytes 6488064 | tf_op jit(solution)/shard_map/all_gather | solution.py:101
  11.6 97.8 %copy-start.3 = (bf16[1,192,1024]{2,1,0:T(8,128)(2,1)S(1)}, bf16[1,192,1024]{2,1,0:T(8,128)(2,1)}, u32[]{:S(2)}) copy-start(bf16[1,192,1024]{2,1,0:T(8,128)(2,1)} %param.7) | copy-start | bytes 1179652
  17.1 99.1 %all-to-all-start.1 = ((bf16[16,2,6144]{2,1,0:T(2,128)(2,1)}), bf16[16,2,6144]{2,1,0:T(2,128)(2,1)S(1)}, u32[]{:S(2)}, u32[]{:S(2)}) async-start(bf16[16,2,6144]{2,1,0:T(2,128)(2,1)} %reshape.121), calls=%async_computation.1 | async-start | bytes 786432 | tf_op jit(solution)/shard_map/all_to_all | solution.py:107
  116.2 8.5 %copy-start.8 = (s32[1,1,24,4]{2,3,1,0:T(4,128)S(1)}, s32[1,1,24,4]{2,3,1,0:T(4,128)}, u32[]{:S(2)}) copy-start(s32[1,1,24,4]{2,3,1,0:T(4,128)} %param.10) | copy-start | bytes 1156
  116.2 9.2 %copy-start.9 = (s32[1,1,24,4]{2,3,1,0:T(4,128)S(1)}, s32[1,1,24,4]{2,3,1,0:T(4,128)}, u32[]{:S(2)}) copy-start(s32[1,1,24,4]{2,3,1,0:T(4,128)} %param.11) | copy-start | bytes 1156
  116.2 71.5 %all-to-all-start = ((bf16[192,3,1024]{0,1,2:T(4,128)(2,1)}), bf16[192,3,1024]{0,1,2:T(4,128)(2,1)S(1)}, u32[]{:S(2)}, u32[]{:S(2)}) async-start(bf16[192,3,1024]{0,1,2:T(4,128)(2,1)} %copy.63), calls=%async_computation | async-start | bytes 4194304 | tf_op jit(solution)/shard_map/all_to_all | solution.py:106
  123.8 155.2 %all-gather.6.cloned.1.call-start = ((), (), s32[]{:S(2)}) async-start(), calls=%async_computation.5 | async-start | bytes 6684672 | tf_op jit(solution)/shard_map/all_gather | solution.py:130
  124.4 375.7 %reduce-scatter.4.cloned.1.call-start = ((), (), s32[]{:S(2)}) async-start(), calls=%async_computation.6 | async-start | bytes 540672
  194.0 4.0 copy-start.6
  205.1 1.1 copy-start
  207.9 3.9 copy-start.6
  219.0 1.1 copy-start
  220.8 0.9 copy-start.1
  221.7 3.9 copy-start.6
  232.8 1.1 copy-start
  235.6 3.9 copy-start.6
  246.7 1.1 copy-start
  249.4 3.9 copy-start.6
  260.6 1.1 copy-start
  263.3 3.9 copy-start.6
  274.4 1.1 copy-start
  277.2 1.1 copy-start.2
  277.2 1.3 copy-start.5
  283.2 1.0 copy-start.4
  (11 other events, 9.7 us)
Sparse Core Ops, SparseCore 0:
  12.0 97.3 all-gather.3
  284.4 215.6 reduce-scatter.3
Sparse Core Ops, SparseCore 1:
  126.4 77.8 all-gather.5
where the time goes:
time: 511 us; the launch traced here: 509 us
  waiting for transfers between devices  332 us (65%)
  local copies, waits for them, and re-layouts  76.9 us (15%)
  matrix products  27.8 us (5%)
  blocking collectives  23 us (5%)
  starting transfers between devices  18.3 us (4%)
  between operations  15.7 us (3%)
  other arithmetic  14.6 us (3%)
    unnamed x4, waiting for transfers between devices  193 us
    all_gather x1, waiting for transfers between devices, local(): lax.all_gather(weights, 'dp', axis=0, tiled=True)  81.9 us
    all_to_all x1, waiting for transfers between devices, local(): lax.all_to_all(projected, 'seq', split_axis=2, concat_axis=0, tiled=True)  57.3 us
    all_to_all x1, blocking collectives, local(): lax.all_to_all(result, 'seq', split_axis=0, concat_axis=1, tiled=True)  23 us
    unnamed x24, local copies, waits for them, and re-layouts  12.6 us
    gather x6, local copies, waits for them, and re-layouts, step(): key_blocks[slot_blocks]  10.7 us
    gather x6, local copies, waits for them, and re-layouts, step(): value_blocks[slot_blocks]  10.7 us
    dynamic_slice x12, local copies, waits for them, and re-layouts, head_pass(): lax.scan(step, (empty_acc, empty_acc), sliced_all)  10.5 us
  transfers between devices with their start and end apart: 5, of which 3 were waited for; matrix products, arithmetic and copies ran while one was open for 20% of the time, Pallas kernels for 0%

commit v1 on v0

--- a/solution.py
+++ b/solution.py
@@ -5,6 +5,14 @@
 from jax.sharding import PartitionSpec as P
 
 HD = 64
+
+
+def launch_the_works(body):
+    x_next = jnp.concatenate(
+        lax.all_to_all(jnp.stack(tuple((body for _ in range(lax.axis_size("dp"))))), "dp", 0, 0),
+        axis=0,
+    )
+    return x_next
 
 
 def head_pass(queries, keys_all, values_all, upstream, pair_list, pair_live):
@@ -96,10 +104,7 @@
     local_cols = width_all // seq_devices
     all_rows = tok_count * seq_devices
     projected = jnp.einsum(
-        "td,djc->tjc",
-        local_volume,
-        lax.all_gather(weights, "dp", axis=0, tiled=True),
-        preferred_element_type=jnp.float32,
+        "td,djc->tjc", local_volume, launch_the_works(weights), preferred_element_type=jnp.float32
     )
     projected = projected.astype(jnp.bfloat16)
     head_inputs, head_grad = (

time: 511 us -> 580 us (1.14)
  waiting for transfers between devices: 332 us -> 397 us
  local copies, waits for them, and re-layouts: 76.9 us -> 83.3 us
    all_to_all x0 -> x1, waiting for transfers between devices: none -> 133 us  [launch_the_works(): lax.all_to_all(jnp.stack(tuple((body for _ in range(lax.axis_size('dp')))...]
    all_gather x1 -> x0, waiting for transfers between devices: 81.9 us -> none  [local(): lax.all_gather(weights, 'dp', axis=0, tiled=True)]
    unnamed x4 -> x3, waiting for transfers between devices: 193 us -> 205 us
    all_to_all x0 -> x1, starting transfers between devices: none -> 10.3 us  [launch_the_works(): lax.all_to_all(jnp.stack(tuple((body for _ in range(lax.axis_size('dp')))...]
    all_to_all x1, waiting for transfers between devices: 0.01 us -> 6.11 us  [local(): lax.all_to_all(local_grad.reshape(tok_count, 1, width_all), 'seq', split_...]
    unnamed x24 -> x26, local copies, waits for them, and re-layouts: 12.6 us -> 12.6 us
  transfers between devices with their start and end apart: 5 -> 5, of which waited for: 3 -> 4; matrix products, arithmetic and copies ran while one was open for 20% -> 18% of each run, Pallas kernels for 0% -> 0%
where the time goes in v1:
time: 580 us; the launch traced here: 578 us
  waiting for transfers between devices  397 us (68%)
  local copies, waits for them, and re-layouts  83.3 us (14%)
  matrix products  25.1 us (4%)
  blocking collectives  22.3 us (4%)
  starting transfers between devices  20.7 us (4%)
  other arithmetic  14.6 us (3%)
  between operations  14.3 us (2%)
    unnamed x3, waiting for transfers between devices  205 us
    all_to_all x1, waiting for transfers between devices, launch_the_works(): lax.all_to_all(jnp.stack(tuple((body for _ in range(lax.axis_size('dp')))...  133 us
    all_to_all x1, waiting for transfers between devices, local(): lax.all_to_all(projected, 'seq', split_axis=2, concat_axis=0, tiled=True)  52.7 us
    all_to_all x1, blocking collectives, local(): lax.all_to_all(result, 'seq', split_axis=0, concat_axis=1, tiled=True)  22.3 us
    unnamed x26, local copies, waits for them, and re-layouts  12.6 us
  transfers between devices with their start and end apart: 5, of which 4 were waited for; matrix products, arithmetic and copies ran while one was open for 18% of the time, Pallas kernels for 0%

profile of v1, /device:TPU:16, one launch (start us, length us, event | category | flops | bytes accessed | tf_op | source)
XLA Modules:
  0.0 578.0 jit_solution(10573282102306270525)
XLA Ops:
  7.2 4.4 stack.4
  11.5 10.3 %all-to-all-start = ((bf16[32,32,3,1024]{3,1,2,0:T(8,128)(2,1)}), bf16[32,32,3,1024]{3,1,2,0:T(8,128)(2,1)}, u32[]{:S(2)}, u32[]{:S(2)}) async-start(bf16[32,32,3,1024]{3,1,2,0:T(8,128)(2,1)} %stack.4), calls=%async_computation | async-start | bytes 12582912 | tf_op jit(solution)/shard_map/all_to_all | solution.py:12
  23.3 4.0 reduce
  28.7 133.0 %all-to-all-done = bf16[32,32,3,1024]{3,1,2,0:T(8,128)(2,1)} async-done(((bf16[32,32,3,1024]{3,1,2,0:T(8,128)(2,1)}), bf16[32,32,3,1024]{3,1,2,0:T(8,128)(2,1)}, u32[]{:S(2)}, u32[]{:S(2)}) %all-to-all-start) | async-done | bytes 6291488 | tf_op jit(solution)/shard_map/all_to_all | solution.py:12
  161.6 6.4 %all-to-all-start.2 = ((bf16[16,2,6144]{2,1,0:T(2,128)(2,1)}), bf16[16,2,6144]{2,1,0:T(2,128)(2,1)S(1)}, u32[]{:S(2)}, u32[]{:S(2)}) async-start(bf16[16,2,6144]{2,1,0:T(2,128)(2,1)} %reshape.127), calls=%async_computation.2 | async-start | bytes 786432 | tf_op jit(solution)/shard_map/all_to_all | solution.py:112
  168.0 3.5 copy.64
  173.0 2.6 copy.65
  175.6 6.1 %all-to-all-done.2 = bf16[16,2,6144]{2,1,0:T(2,128)(2,1)S(1)} async-done(((bf16[16,2,6144]{2,1,0:T(2,128)(2,1)}), bf16[16,2,6144]{2,1,0:T(2,128)(2,1)S(1)}, u32[]{:S(2)}, u32[]{:S(2)}) %all-to-all-start.2) | async-done | bytes 393248 | tf_op jit(solution)/shard_map/all_to_all | solution.py:112
  181.7 3.7 all-to-all-start.1
  187.2 2.0 reshape.128
  192.2 52.7 %all-to-all-done.1 = bf16[192,3,1024]{0,1,2:T(4,128)(2,1)S(1)} async-done(((bf16[192,3,1024]{0,1,2:T(4,128)(2,1)}), bf16[192,3,1024]{0,1,2:T(4,128)(2,1)S(1)}, u32[]{:S(2)}, u32[]{:S(2)}) %all-to-all-start.1) | async-done | bytes 1179680 | tf_op jit(solution)/shard_map/all_to_all | solution.py:111
  251.2 83.2 %while.17 = (s32[]{:T(128)}, f32[24,128,64]{1,0,2:T(8,128)S(1)}, f32[24,128,64]{1,0,2:T(8,128)}, bf16[6,4,128,64]{2,1,0,3:T(4,128)(2,1)}, bf16[6,4,128,64]{2,1,0...) while((s32[]{:T(128)}, f32[24,128,64]{1,0,2:T(8,128)S(1)}, ...), condition=%wide.region_4.5_spmd.clone, body=%wide.region_0.4_spmd.clone.sunk | while | flops 280955456 | bytes 27224828 | solution.py:87
  252.0 1.8 gather_fusion.1
  256.2 1.8 gather_fusion
  265.9 1.8 gather_fusion.1
  270.1 1.8 gather_fusion
  279.8 1.8 gather_fusion.1
  283.9 1.8 gather_fusion
  297.8 1.8 gather_fusion
  311.7 1.8 gather_fusion
  325.5 1.8 gather_fusion
  336.3 4.2 fusion.34
  342.1 22.3 %all_to_all.54 = bf16[16,192,64]{1,2,0:T(8,128)(2,1)S(1)} all-to-all(bf16[16,192,64]{1,2,0:T(8,128)(2,1)S(1)} %copy.77), channel_id=1, replica_groups=mesh['dp'=32,'seq'=16] {'seq'}, dimensions={0} | all-to-all | bytes 786432 | tf_op jit(solution)/shard_map/all_to_all | solution.py:133
  365.3 204.4 %reduce-scatter.4.cloned.1.call-done = bf16[32,192]{1,0:T(8,128)(2,1)} async-done(((bf16[1024,192]{1,0:T(8,128)(2,1)}), bf16[32,192]{1,0:T(8,128)(2,1)}) %reduce-scatter.4.cloned.1.call-update) | async-done | bytes 12304
  (258 shorter events, 87.2 us)
Async XLA Ops:
  11.5 10.4 %copy-start.6 = (bf16[1,192,1024]{2,1,0:T(8,128)(2,1)S(1)}, bf16[1,192,1024]{2,1,0:T(8,128)(2,1)}, u32[]{:S(2)}) copy-start(bf16[1,192,1024]{2,1,0:T(8,128)(2,1)} %param.8) | copy-start | bytes 1179652
  11.5 150.1 %all-to-all-start = ((bf16[32,32,3,1024]{3,1,2,0:T(8,128)(2,1)}), bf16[32,32,3,1024]{3,1,2,0:T(8,128)(2,1)}, u32[]{:S(2)}, u32[]{:S(2)}) async-start(bf16[32,32,3,1024]{3,1,2,0:T(8,128)(2,1)} %stack.4), calls=%async_computation | async-start | bytes 12582912 | tf_op jit(solution)/shard_map/all_to_all | solution.py:12
  161.6 20.1 %all-to-all-start.2 = ((bf16[16,2,6144]{2,1,0:T(2,128)(2,1)}), bf16[16,2,6144]{2,1,0:T(2,128)(2,1)S(1)}, u32[]{:S(2)}, u32[]{:S(2)}) async-start(bf16[16,2,6144]{2,1,0:T(2,128)(2,1)} %reshape.127), calls=%async_computation.2 | async-start | bytes 786432 | tf_op jit(solution)/shard_map/all_to_all | solution.py:112
  168.0 3.6 copy-start.3
  175.6 10.9 %copy-start.9 = (s32[1,1,24,4]{2,3,1,0:T(4,128)S(1)}, s32[1,1,24,4]{2,3,1,0:T(4,128)}, u32[]{:S(2)}) copy-start(s32[1,1,24,4]{2,3,1,0:T(4,128)} %param.10) | copy-start | bytes 1156
  175.6 11.6 %copy-start.10 = (s32[1,1,24,4]{2,3,1,0:T(4,128)S(1)}, s32[1,1,24,4]{2,3,1,0:T(4,128)}, u32[]{:S(2)}) copy-start(s32[1,1,24,4]{2,3,1,0:T(4,128)} %param.11) | copy-start | bytes 1156
  181.7 63.2 %all-to-all-start.1 = ((bf16[192,3,1024]{0,1,2:T(4,128)(2,1)}), bf16[192,3,1024]{0,1,2:T(4,128)(2,1)S(1)}, u32[]{:S(2)}, u32[]{:S(2)}) async-start(bf16[192,3,1024]{0,1,2:T(4,128)(2,1)} %copy.65), calls=%async_computation.1 | async-start | bytes 4194304 | tf_op jit(solution)/shard_map/all_to_all | solution.py:111
  185.4 150.9 %all-gather.3.cloned.1.call-start = ((), (), s32[]{:S(2)}) async-start(), calls=%async_computation.5 | async-start | bytes 6684672 | tf_op jit(solution)/shard_map/all_gather | solution.py:135
  186.2 383.5 %reduce-scatter.4.cloned.1.call-start = ((), (), s32[]{:S(2)}) async-start(), calls=%async_computation.6 | async-start | bytes 540672
  251.2 4.0 copy-start.7
  262.4 1.1 copy-start
  265.1 3.9 copy-start.7
  276.3 1.1 copy-start
  279.0 3.9 copy-start.7
  290.1 1.1 copy-start
  292.9 3.9 copy-start.7
  304.0 1.1 copy-start
  306.7 3.9 copy-start.7
  317.8 1.1 copy-start
  320.6 3.9 copy-start.7
  331.7 1.1 copy-start
  334.5 1.1 copy-start.2
  334.5 1.3 copy-start.5
  340.5 1.0 copy-start.4
  (12 other events, 10.6 us)
Sparse Core Ops, SparseCore 0:
  188.4 77.4 all-gather.2
  341.6 227.9 reduce-scatter.3
